TPU v7x, 32 devices: a whole 2x2x4 slice. The times are simulated.
32 devices in a mesh: dp: 16 (over z, y, x), head: 2 (over core).
Axes of the slice: x: 2, y: 2, z: 4, core: 2. Of those that a mesh axis runs over, the one named last changes fastest.
Arguments:
- latents: bfloat16 [32768, 1280], P('dp'), may hold values from -6 to 6
- languages: int32 [128], P('dp'), may hold values from 0 to 15, never falling along the last dimension, each value on 1 to 64 neighbouring positions
- lang_table: bfloat16 [16, 1280], replicated, may hold values from -3 to 3
- norm1_gain: float32 [1280], replicated, may hold values from 0.5 to 1.5
- norm1_shift: float32 [1280], replicated, may hold values from -2 to 2
- qkv_weight: bfloat16 [1280, 3, 1280], P(None, None, 'head'), may hold values from -0.15625 to 0.15625
- out_weight: bfloat16 [1280, 1280], P('head'), may hold values from -2.5 to 2.5
- out_bias: float32 [1280], replicated, may hold values from -2 to 2
- norm2_gain: float32 [1280], replicated, may hold values from 0.5 to 1.5
- norm2_shift: float32 [1280], replicated, may hold values from -2 to 2
- up_weight: bfloat16 [1280, 1280], P(None, 'head'), may hold values from -0.15625 to 0.15625
- up_bias: float32 [1280], P('head'), may hold values from -3 to 3
- down_weight: bfloat16 [1280, 1280], P('head'), may hold values from -0.25 to 0.25
- down_bias: float32 [1280], replicated, may hold values from -2 to 2
- cotangent: bfloat16 [32768, 1280], P('dp'), may hold values from -6 to 6
Outputs:
- block_out: bfloat16 [32768, 1280], P(('dp', 'head'))
- input_grad: float32 [32768, 1280], P(('dp', 'head'))
- table_grad: float32 [16, 1280], replicated
- norm1_gain_grad: float32 [1280], replicated
- norm1_shift_grad: float32 [1280], replicated
- qkv_grad: float32 [1280, 3, 1280], P(None, None, 'head')
- out_weight_grad: float32 [1280, 1280], P('head')
- out_bias_grad: float32 [1280], replicated
- norm2_gain_grad: float32 [1280], replicated
- norm2_shift_grad: float32 [1280], replicated
- up_weight_grad: float32 [1280, 1280], P(None, 'head')
- up_bias_grad: float32 [1280], P('head')
- down_weight_grad: float32 [1280, 1280], P('head')
- down_bias_grad: float32 [1280], replicated
Inputs may be any that keep to these rules, and one draw needn't show every extreme that they name: `languages`: ids never fall from one item to the next; every language has at least one item.
All inputs are finite; a program needn't handle non-finite values.
Results may differ from a plain program's by a relative error of at most 0.015.
Values may be sent and summed in bfloat16 or wider, within the bound.
No kernel may reach another device: no remote copies, remote signals or barrier semaphores. Data moves between devices by JAX's collectives and lax.ppermute only.
A program may use at most 256 MiB of HBM per device.

v0:
```python
from functools import partial

import jax
import jax.numpy as jnp
from jax import lax
from jax.sharding import PartitionSpec as P

HEAD_DIM = 160


EPS = 1e-05
HIGH = lax.Precision.HIGHEST


def normalize(values, gain, shift):
    mean = jnp.mean(values, axis=-1, keepdims=True)
    centred = values - mean
    inverse = lax.rsqrt(jnp.mean(centred * centred, axis=-1, keepdims=True) + EPS)
    unit = centred * inverse
    return (unit * gain + shift, unit, inverse)


def normalize_back(grad, unit, inverse, gain):
    scaled = grad * gain
    return inverse * (
        scaled
        - jnp.mean(scaled, axis=-1, keepdims=True)
        - unit * jnp.mean(scaled * unit, axis=-1, keepdims=True)
    )


def own_rows(values, start, share):
    return lax.dynamic_slice_in_dim(values, start, share, 0)


def body(
    latents,
    languages,
    lang_table,
    norm1_gain,
    norm1_shift,
    qkv_weight,
    out_weight,
    out_bias,
    norm2_gain,
    norm2_shift,
    up_weight,
    up_bias,
    down_weight,
    down_bias,
    cotangent,
):
    f32 = jnp.float32
    bf16 = jnp.bfloat16
    items = languages.shape[0]
    rows = latents.shape[0]
    span = rows // items
    width = latents.shape[1]
    local = qkv_weight.shape[2]
    heads_here = local // HEAD_DIM
    scale = HEAD_DIM ** (-0.5)
    share = rows // lax.axis_size("head")
    start = lax.axis_index("head") * share
    token_lang = jnp.repeat(languages, span)
    onehot = (
        token_lang[:, None] == jnp.arange(lang_table.shape[0], dtype=jnp.int32)[None, :]
    ).astype(bf16)
    base = latents.astype(f32) + jnp.dot(onehot, lang_table, preferred_element_type=f32)
    normed1, unit1, inverse1 = normalize(base, norm1_gain, norm1_shift)
    h_one = normed1.astype(bf16)
    qkv_flat = qkv_weight.reshape(width, 3 * local)
    proj = jnp.dot(h_one, qkv_flat, preferred_element_type=f32).astype(bf16)
    proj = proj.reshape(items, span, 3, heads_here, HEAD_DIM)
    query = proj[:, :, 0]
    key = proj[:, :, 1]
    value = proj[:, :, 2]
    raw = jnp.einsum("iqhd,ikhd->ihqk", query, key, preferred_element_type=f32) * scale
    peak = jnp.max(raw, axis=-1, keepdims=True)
    weights = jnp.exp(raw - peak)
    probs = weights / jnp.sum(weights, axis=-1, keepdims=True)
    probs_low = probs.astype(bf16)
    mixed = jnp.einsum("ihqk,ikhd->iqhd", probs_low, value, preferred_element_type=f32)
    mixed = mixed.astype(bf16).reshape(rows, local)
    attn_part = jnp.dot(mixed, out_weight, preferred_element_type=f32)
    attn_full = lax.psum(attn_part, "head")
    middle = base + attn_full + out_bias
    normed2, unit2, inverse2 = normalize(middle, norm2_gain, norm2_shift)
    h_two = normed2.astype(bf16)
    pre = jnp.dot(h_two, up_weight, preferred_element_type=f32) + up_bias
    act, gelu_back = jax.vjp(partial(jax.nn.gelu, approximate=True), pre)
    act_low = act.astype(bf16)
    down_part = jnp.dot(act_low, down_weight, preferred_element_type=f32)
    final = (
        middle + lax.psum(down_part.astype(jnp.bfloat16), "head").astype(jnp.float32) + down_bias
    )
    block_out = own_rows(final, start, share).astype(bf16)
    grad_rows = cotangent.astype(f32)
    d_act = jnp.einsum("td,fd->tf", cotangent, down_weight, preferred_element_type=f32)
    d_down = jnp.einsum("tf,td->fd", act_low, cotangent, preferred_element_type=f32)
    d_pre_low = gelu_back(d_act)[0].astype(bf16)
    d_up = jnp.einsum("td,tf->df", h_two, d_pre_low, preferred_element_type=f32)
    d_up_bias = jnp.sum(d_pre_low.astype(f32), axis=0)
    h2_part = jnp.einsum("tf,df->td", d_pre_low, up_weight, preferred_element_type=f32)
    h2_grad = lax.psum(h2_part, "head")
    d_middle = grad_rows + normalize_back(h2_grad, unit2, inverse2, norm2_gain)
    d_middle_low = d_middle.astype(bf16)
    d_gain2 = jnp.sum(h2_grad * unit2, axis=0)
    d_shift2 = jnp.sum(h2_grad, axis=0)
    d_out_bias = jnp.sum(d_middle, axis=0)
    d_down_bias = jnp.sum(grad_rows, axis=0)
    d_out = jnp.einsum("tc,td->cd", mixed, d_middle_low, preferred_element_type=f32)
    d_mixed = jnp.einsum("td,cd->tc", d_middle_low, out_weight, preferred_element_type=f32)
    d_mixed = d_mixed.astype(bf16).reshape(items, span, heads_here, HEAD_DIM)
    d_probs = jnp.einsum("iqhd,ikhd->ihqk", d_mixed, value, preferred_element_type=f32)
    d_value = jnp.einsum("ihqk,iqhd->ikhd", probs_low, d_mixed, preferred_element_type=f32)
    d_raw = probs * (d_probs - jnp.sum(probs * d_probs, axis=-1, keepdims=True))
    d_raw_low = d_raw.astype(bf16)
    d_query = jnp.einsum("ihqk,ikhd->iqhd", d_raw_low, key, preferred_element_type=f32) * scale
    d_key = jnp.einsum("ihqk,iqhd->ikhd", d_raw_low, query, preferred_element_type=f32) * scale
    d_proj = jnp.stack([d_query, d_key, d_value], axis=2).astype(bf16).reshape(rows, 3 * local)
    d_qkv = jnp.einsum("td,tc->dc", h_one, d_proj, preferred_element_type=f32).reshape(
        width, 3, local
    )
    h1_part = jnp.einsum("tc,dc->td", d_proj, qkv_flat, preferred_element_type=f32)
    h1_grad = lax.psum(h1_part.astype(jnp.bfloat16), "head").astype(jnp.float32)
    d_base = d_middle + normalize_back(h1_grad, unit1, inverse1, norm1_gain)
    onehot_own = onehot.astype(f32)
    input_grad = own_rows(d_base, start, share)
    d_gain1 = jnp.sum(h1_grad * unit1, axis=0)
    d_shift1 = jnp.sum(h1_grad, axis=0)
    d_table = jnp.einsum("tl,td->ld", onehot_own, d_base, precision=HIGH)
    (
        d_qkv,
        d_out,
        d_up,
        d_up_bias,
        d_down,
        d_table,
        d_gain1,
        d_shift1,
        d_out_bias,
        d_gain2,
        d_shift2,
        d_down_bias,
    ) = (
        lax.psum(d_qkv.astype(jnp.bfloat16), "dp").astype(jnp.float32),
        lax.psum(d_out.astype(jnp.bfloat16), "dp").astype(jnp.float32),
        lax.psum(d_up.astype(jnp.bfloat16), "dp").astype(jnp.float32),
        lax.psum(d_up_bias.astype(jnp.bfloat16), "dp").astype(jnp.float32),
        lax.psum(d_down.astype(jnp.bfloat16), "dp").astype(jnp.float32),
        lax.psum(d_table.astype(jnp.bfloat16), "dp").astype(jnp.float32),
        lax.psum(d_gain1.astype(jnp.bfloat16), "dp").astype(jnp.float32),
        lax.psum(d_shift1.astype(jnp.bfloat16), "dp").astype(jnp.float32),
        lax.psum(d_out_bias.astype(jnp.bfloat16), "dp").astype(jnp.float32),
        lax.psum(d_gain2.astype(jnp.bfloat16), "dp").astype(jnp.float32),
        lax.psum(d_shift2.astype(jnp.bfloat16), "dp").astype(jnp.float32),
        lax.psum(d_down_bias.astype(jnp.bfloat16), "dp").astype(jnp.float32),
    )
    return (
        block_out,
        input_grad,
        d_table,
        d_gain1,
        d_shift1,
        d_qkv,
        d_out,
        d_out_bias,
        d_gain2,
        d_shift2,
        d_up,
        d_up_bias,
        d_down,
        d_down_bias,
    )


def solution(mesh):
    in_specs = (
        P("dp", None),
        P("dp"),
        P(),
        P(),
        P(),
        P(None, None, "head"),
        P("head", None),
        P(),
        P(),
        P(),
        P(None, "head"),
        P("head"),
        P("head", None),
        P(),
        P("dp", None),
    )
    out_specs = (
        P(("dp", "head"), None),
        P(("dp", "head"), None),
        P(),
        P(),
        P(),
        P(None, None, "head"),
        P("head", None),
        P(),
        P(),
        P(),
        P(None, "head"),
        P("head"),
        P("head", None),
        P(),
    )
    return jax.shard_map(body, mesh=mesh, in_specs=in_specs, out_specs=out_specs, check_vma=False)
```

profile of v0, /device:TPU:0, one launch (start us, length us, event | category | flops | bytes accessed | tf_op | source)
XLA Modules:
  0.0 835.3 jit_solution(8268449116038774640)
XLA Ops:
  8.1 8.2 copy.47
  16.3 7.9 copy.46
  32.8 16.7 %convolution_convert_fusion.2 = bf16[2048,1920]{1,0:T(8,128)(2,1)} fusion(bf16[1280,1920]{0,1:T(8,128)(2,1)S(1)} %bitcast.99, f32[2048,1280]{0,1:T(8,128)} %copy-done.1, f32[1280]{0:T(1024)S(1)} %copy-done.39, f32[1280]{0:T(1024)S(1)} %copy-done.27, f32[2048]{0:T(1024)S(1)} %add_rsqrt_fusion.1, f32[2048]{0:T(1024)S(1)} %broadcast_multiply_fusion.5), kind=kOutput, calls=%fused_computation.29 | convolution fusion | flops 10083368960 | bytes 23291904 | tf_op jit(solution)/shard_map/dot_general | solution.py:72
  49.5 23.8 %reshape.108 = bf16[8,256,3,4,160]{4,3,2,1,0:T(4,128)(2,1)} reshape(bf16[2048,1920]{1,0:T(8,128)(2,1)} %convolution_convert_fusion.2) | data formatting | bytes 15728640 | tf_op jit(solution)/shard_map/reshape | solution.py:73
  73.4 10.1 %fusion.59 = (bf16[8,256,1,4,160]{4,3,2,1,0:T(4,128)(2,1)}, bf16[8,256,1,4,160]{4,3,2,1,0:T(4,128)(2,1)}, bf16[8,256,1,4,160]{4,3,2,1,0:T(4,128)(2,1)}) fusion(bf16[8,256,3,4,160]{4,3,2,1,0:T(4,128)(2,1)} %reshape.108), kind=kLoop, calls=%fused_computation.92 | loop fusion | bytes 15728640 | tf_op jit(solution)/shard_map/slice | solution.py:74
  83.5 7.1 copy.81
  90.6 7.1 copy.80
  97.7 7.6 copy.82
  129.7 45.5 %all-reduce.8.cloned.1.call-done = f32[2048,1280]{0,1:T(8,128)} async-done(((f32[2048,1280]{0,1:T(8,128)}), f32[2048,1280]{0,1:T(8,128)}) %all-reduce.8.cloned.1.call-update) | async-done | bytes 10485776 | tf_op jit(solution)/shard_map/psum | solution.py:85
  175.1 8.0 fusion.58
  191.0 6.8 fusion.63
  197.9 11.2 %fusion.55 = (bf16[640]{0:T(1024)(128)(2,1)}, bf16[2048,640]{1,0:T(8,128)(2,1)S(1)}) fusion(f32[2048,640]{1,0:T(8,128)S(1)} %fusion.63, f32[640]{0:T(1024)S(1)} %copy-done.41, bf16[2048,1280]{1,0:T(8,128)(2,1)} %param.29, bf16[640,1280]{1,0:T(8,128)(2,1)S(1)} %copy-done), kind=kOutput, calls=%fused_computation.89 | convolution fusion | flops 3384278528 | bytes 14749440 | tf_op jit(solution)/shard_map/td,fd->tf/dot_general | solution.py:98
  217.5 8.3 copy.56
  225.8 10.2 %convolution_convert_fusion.4 = bf16[1280,640]{1,0:T(8,128)(2,1)} fusion(bf16[2048,1280]{0,1:T(8,128)(2,1)} %add_convert_fusion, bf16[2048,640]{1,0:T(8,128)(2,1)} %copy-done.42), kind=kOutput, calls=%fused_computation.53 | convolution fusion | flops 3356262400 | bytes 9502720 | tf_op jit(solution)/shard_map/td,tf->df/dot_general | solution.py:101
  236.1 8.2 convolution_convert_fusion.3
  244.3 17.3 %all-reduce.10.cloned.1.call-done = f32[2048,1280]{0,1:T(8,128)} async-done(((f32[2048,1280]{0,1:T(8,128)}), f32[2048,1280]{0,1:T(8,128)}) %all-reduce.10.cloned.1.call-update) | async-done | bytes 10485776 | tf_op jit(solution)/shard_map/psum | solution.py:104
  261.6 10.6 %multiply_reduce_fusion = (bf16[1280]{0:T(1024)(128)(2,1)}, f32[2048]{0:T(1024)S(1)}, f32[2048]{0:T(1024)S(1)}, bf16[1280]{0:T(1024)(128)(2,1)}) fusion(f32[2048,1280]{0,1:T(8,128)} %all-reduce.10.cloned.1.call-done, f32[2048,1280]{0,1:T(8,128)} %copy-done.2, f32[2048]{0:T(1024)S(1)} %add_rsqrt_fusion, f32[2048]{0:T(1024)S(1)} %broadcast_multiply_fusion.4, ...), kind=kLoop, calls=%fused_computation.12 | loop fusion | flops 23586304 | bytes 21014528 | tf_op jit(solution)/shard_map/reduce_sum | solution.py:107
  273.1 8.4 %fusion.57 = (bf16[1280]{0:T(1024)(128)(2,1)}, f32[2048,1280]{0,1:T(8,128)S(1)}) fusion(f32[2048]{0:T(1024)S(1)} %broadcast_multiply_fusion.2, f32[2048,1280]{0,1:T(8,128)} %copy-done.2, f32[2048]{0:T(1024)S(1)} %broadcast_multiply_fusion.4, f32[2048]{0:T(1024)S(1)} %broadcast_multiply_fusion.3, f32[2048,1280]{0,1:T(8,128)S(1)} %copy-done.6, ...), kind=kLoop, calls=%fused_computation.90 | loop fusion | flops 26213120 | bytes 36740608 | tf_op jit(solution)/shard_map/reduce_sum | solution.py:109
  292.3 9.1 %reshape.109 = bf16[8,256,4,160]{3,2,1,0:T(4,128)(2,1)} reshape(bf16[2048,640]{1,0:T(8,128)(2,1)} %convolution_convert_fusion.6) | data formatting | bytes 5242880 | tf_op jit(solution)/shard_map/reshape | solution.py:113
  301.4 7.1 copy.59
  308.5 7.4 convolution_bitcast_fusion
  315.9 7.2 multiply_reduce_fusion.5
  329.5 8.5 %copy.64 = bf16[8,256,3,4,160]{1,0,4,3,2:T(8,128)(2,1)} copy(bf16[8,256,3,4,160]{1,4,3,0,2:T(8,128)(2,1)S(1)} %maximum_convert_fusion) | data formatting | bytes 15728640 | tf_op jit(solution)/shard_map/convert_element_type | solution.py:120
  348.0 15.4 %fusion.23 = bf16[1280,3,640]{2,0,1:T(8,128)(2,1)} fusion(bf16[3,640,2048]{2,1,0:T(8,128)(2,1)S(1)} %bitcast.92, f32[2048,1280]{0,1:T(8,128)} %copy-done.1, f32[1280]{0:T(1024)S(1)} %copy-done.40, f32[1280]{0:T(1024)S(1)} %copy-done.28, f32[2048]{0:T(1024)S(1)} %copy-done.25, f32[2048]{0:T(1024)S(1)} %copy-done.22), kind=kOutput, calls=%fused_computation.49 | convolution fusion | flops 10081894400 | bytes 23291904 | tf_op jit(solution)/shard_map/td,tc->dc/dot_general | solution.py:121
  363.4 9.9 %convolution_convert_fusion.1 = bf16[2048,1280]{0,1:T(8,128)(2,1)} fusion(bf16[640,1280]{1,0:T(8,128)(2,1)S(1)} %copy-done, f32[2048,640]{1,0:T(8,128)} %copy-done.43, f32[640]{0:T(1024)S(1)} %copy-done.41), kind=kOutput, calls=%fused_computation.28 | convolution fusion | flops 3371171840 | bytes 12126720 | tf_op jit(solution)/shard_map/dot_general | solution.py:92
  373.4 15.1 %convolution_convert_fusion = bf16[2048,1280]{0,1:T(8,128)(2,1)} fusion(bf16[2048,1920]{0,1:T(8,128)(2,1)S(1)} %bitcast.93, bf16[1280,1920]{0,1:T(8,128)(2,1)} %bitcast.96), kind=kOutput, calls=%fused_computation.27 | convolution fusion | flops 10068951040 | bytes 18022400 | tf_op jit(solution)/shard_map/tc,dc->td/dot_general | solution.py:124
  391.8 264.4 %all-reduce.12.cloned.1.call-done = (bf16[1280,3,640]{2,0,1:T(8,128)(2,1)}, bf16[640,1280]{1,0:T(8,128)(2,1)}, bf16[1280,640]{1,0:T(8,128)(2,1)}, bf16[640,1280]{1,0:T(8,128)(2,1)}) async-done(((bf16[1280,3,640]{2,0,1:T(8,128)(2,1)}, bf16[640,1280]{1,0:T(8,128)(2,1)}, bf16[1280,640]{1,0:T(8,128)(2,1)}, bf16[640,1280]{1,0:T(8,128)(2,1)}), (bf16[1280,3,640]{2,0,1:T(8,128)(2,1)}, bf16[640,1280]{1,0:T(8,128)(2,1)}, ...) | async-done | bytes 9830416 | tf_op jit(solution)/shard_map/psum | solution.py:146
  669.1 32.0 %all-reduce.14.cloned.1.call-done = (bf16[2048,1280]{0,1:T(8,128)(2,1)}, bf16[2048,1280]{0,1:T(8,128)(2,1)}) async-done(((bf16[2048,1280]{0,1:T(8,128)(2,1)}, bf16[2048,1280]{0,1:T(8,128)(2,1)}), (bf16[2048,1280]{0,1:T(8,128)(2,1)}, bf16[2048,1280]{0,1:T(8,128)(2,1)})) %all-reduce.14.cloned.1.call-update) | async-done | bytes 10485776 | tf_op jit(solution)/shard_map/psum | solution.py:94
  704.3 8.1 fusion.8
  712.5 9.9 %fusion.6 = f32[2048,1280]{0,1:T(8,128)S(1)} fusion(f32[2048,1280]{0,1:T(8,128)} %copy-done.5, bf16[2048,1280]{0,1:T(8,128)(2,1)S(1)} %copy-done.4, f32[2048,1280]{0,1:T(8,128)} %copy-done.1, f32[2048]{0:T(1024)S(1)} %broadcast_multiply_fusion, f32[2048]{0:T(1024)S(1)} %broadcast_multiply_fusion.1, f32[1280]{0:T(1024)S(1)} %copy-done.28, ...), kind=kLoop, calls=%fused_computation.9 | loop fusion | flops 23592960 | bytes 36738048 | tf_op jit(solution)/shard_map/add | solution.py:126
  727.8 7.4 fusion.20
  739.6 78.0 %all-reduce = (bf16[16,1280]{1,0:T(8,128)(2,1)S(1)}, bf16[1280]{0:T(1024)(128)(2,1)S(1)}, bf16[1280]{0:T(1024)(128)(2,1)S(1)}, bf16[1280]{0:T(1024)(128)(2,1)S(1...) all-reduce(bf16[16,1280]{1,0:T(8,128)(2,1)S(1)} %convolution_conver, ...), channel_id=1, replica_groups=mesh['dp'=16,'head'=2] {'dp'}, use_global_device_ids=true, to_apply=%region_15.0 | all-reduce | flops 28800 | bytes 115200 | tf_op jit(solution)/shard_map/psum | solution.py:151
  (168 shorter events, 117.9 us)
Async XLA Ops:
  7.2 190.7 %copy-start = (bf16[640,1280]{1,0:T(8,128)(2,1)S(1)}, bf16[640,1280]{1,0:T(8,128)(2,1)}, u32[]{:S(2)}) copy-start(bf16[640,1280]{1,0:T(8,128)(2,1)} %param.27) | copy-start | bytes 4915204
  7.2 167.9 %all-reduce.8.cloned.1.call-start = ((), (), s32[]{:S(2)}) async-start(), calls=%async_computation | async-start | bytes 20971520 | tf_op jit(solution)/shard_map/psum | solution.py:85
  8.1 16.1 %copy-start.19 = (s32[1,2,8,128]{3,1,2,0:T(2,128)}, s32[1,2,8,128]{3,1,2,0:T(2,128)S(1)}, u32[]{:S(2)}) copy-start(s32[1,2,8,128]{3,1,2,0:T(2,128)S(1)} %copy.83) | copy-start | bytes 24580
  16.3 8.0 copy-start.26
  16.3 16.5 %slice-start.9 = ((s8[4915200]{0:T(1024)(128)(4,1)}), s8[720896]{0:T(1024)(128)(4,1)S(1)}, s32[]{:S(2)}) async-start(s8[4915200]{0:T(1024)(128)(4,1)} %bitcast.97), calls=%async_computation.13 | async-start | bytes 1441792
  24.2 8.6 %slice-start.10 = ((s8[4915200]{0:T(1024)(128)(4,1)}), s8[4194304]{0:T(1024)(128)(4,1)S(1)}, s32[]{:S(2)}) async-start(s8[4915200]{0:T(1024)(128)(4,1)} %bitcast.97), calls=%async_computation.14 | async-start | bytes 8388608
  109.1 6.3 copy-start.13
  129.6 45.6 %copy-start.32 = (f32[1280]{0:T(1024)S(1)}, f32[1280]{0:T(1024)}, u32[]{:S(2)}) copy-start(f32[1280]{0:T(1024)} %param.22) | copy-start | bytes 15364
  129.6 132.0 %all-reduce.10.cloned.1.call-start = ((), (), s32[]{:S(2)}) async-start(), calls=%async_computation.1 | async-start | bytes 20971520 | tf_op jit(solution)/shard_map/psum | solution.py:104
  191.0 6.9 copy-start.41
  197.9 11.3 %copy-start.43 = (f32[2048,640]{1,0:T(8,128)}, f32[2048,640]{1,0:T(8,128)S(1)}, u32[]{:S(2)}) copy-start(f32[2048,640]{1,0:T(8,128)S(1)} %fusion.63) | copy-start | bytes 15728644
  197.9 12.8 %copy-start.36 = (bf16[1280,640]{1,0:T(8,128)(2,1)S(1)}, bf16[1280,640]{1,0:T(8,128)(2,1)}, u32[]{:S(2)}) copy-start(bf16[1280,640]{1,0:T(8,128)(2,1)} %param.25) | copy-start | bytes 4915204
  217.5 438.7 %all-reduce.12.cloned.1.call-start = ((), (), s32[]{:S(2)}) async-start(), calls=%async_computation.2 | async-start | bytes 19660800 | tf_op jit(solution)/shard_map/psum | solution.py:146
  217.5 18.5 %slice-start.5 = ((s8[5242880]{0:T(1024)(128)(4,1)}), s8[1048576]{0:T(1024)(128)(4,1)S(1)}, s32[]{:S(2)}) async-start(s8[5242880]{0:T(1024)(128)(4,1)} %bitcast.89), calls=%async_computation.9 | async-start | bytes 2097152
  225.8 10.2 %slice-start.6 = ((s8[5242880]{0:T(1024)(128)(4,1)}), s8[4194304]{0:T(1024)(128)(4,1)S(1)}, s32[]{:S(2)}) async-start(s8[5242880]{0:T(1024)(128)(4,1)} %bitcast.89), calls=%async_computation.10 | async-start | bytes 8388608
  261.6 10.6 %copy-start.6 = (f32[2048,1280]{0,1:T(8,128)S(1)}, f32[2048,1280]{0,1:T(8,128)}, u32[]{:S(2)}) copy-start(f32[2048,1280]{0,1:T(8,128)} %all-reduce.10.cloned.1.call-done) | copy-start | bytes 31457284
  261.6 11.5 %copy-start.10 = (bf16[2048,1280]{0,1:T(8,128)(2,1)S(1)}, bf16[2048,1280]{0,1:T(8,128)(2,1)}, u32[]{:S(2)}) copy-start(bf16[2048,1280]{0,1:T(8,128)(2,1)} %copy.56) | copy-start | bytes 15728644
  273.1 8.5 %copy-start.15 = (bf16[80,8,8,256]{3,1,2,0:T(8,128)(2,1)S(1)}, bf16[80,8,8,256]{3,1,2,0:T(8,128)(2,1)}, u32[]{:S(2)}) copy-start(bf16[80,8,8,256]{3,1,2,0:T(8,128)(2,1)} %copy-done.14) | copy-start | bytes 7864324
  308.5 14.6 %slice-start.3 = ((s8[8388608]{0:T(1024)(128)(4,1)}), s8[4194304]{0:T(1024)(128)(4,1)S(1)}, s32[]{:S(2)}) async-start(s8[8388608]{0:T(1024)(128)(4,1)} %bitcast.86), calls=%async_computation.7 | async-start | bytes 8388608
  315.9 7.2 slice-start.4
  338.0 10.0 %copy-start.22 = (f32[2048]{0:T(1024)S(1)}, f32[2048]{0:T(1024)}, u32[]{:S(2)}) copy-start(f32[2048]{0:T(1024)} %copy-done.21) | copy-start | bytes 24580
  338.0 10.0 %copy-start.25 = (f32[2048]{0:T(1024)S(1)}, f32[2048]{0:T(1024)}, u32[]{:S(2)}) copy-start(f32[2048]{0:T(1024)} %copy-done.24) | copy-start | bytes 24580
  338.0 10.0 %copy-start.28 = (f32[1280]{0:T(1024)S(1)}, f32[1280]{0:T(1024)}, u32[]{:S(2)}) copy-start(f32[1280]{0:T(1024)} %param.18) | copy-start | bytes 15364
  338.0 10.0 %copy-start.40 = (f32[1280]{0:T(1024)S(1)}, f32[1280]{0:T(1024)}, u32[]{:S(2)}) copy-start(f32[1280]{0:T(1024)} %param.19) | copy-start | bytes 15364
  363.4 337.7 %all-reduce.14.cloned.1.call-start = ((), (), s32[]{:S(2)}) async-start(), calls=%async_computation.3 | async-start | bytes 20971520 | tf_op jit(solution)/shard_map/psum | solution.py:94
  363.4 9.9 %copy-start.12 = (bf16[240,8,8,256]{3,1,2,0:T(8,128)(2,1)S(1)}, bf16[240,8,8,256]{3,1,2,0:T(8,128)(2,1)}, u32[]{:S(2)}) copy-start(bf16[240,8,8,256]{3,1,2,0:T(8,128)(2,1)} %copy-done.11) | copy-start | bytes 23592964
  656.2 7.4 slice-start.7
  704.3 8.1 copy-start.4
  704.3 23.4 %slice-start = ((s8[10485760]{0:T(1024)(128)(4,1)}), s8[4194304]{0:T(1024)(128)(4,1)S(1)}, s32[]{:S(2)}) async-start(s8[10485760]{0:T(1024)(128)(4,1)} %bitcast.84), calls=%async_computation.4 | async-start | bytes 8388608
  712.5 10.0 %copy-start.20 = (s32[1,2,8,128]{3,1,2,0:T(2,128)S(1)}, s32[1,2,8,128]{3,1,2,0:T(2,128)}, u32[]{:S(2)}) copy-start(s32[1,2,8,128]{3,1,2,0:T(2,128)} %copy-done.19) | copy-start | bytes 24580
  712.5 15.3 %slice-start.1 = ((s8[10485760]{0:T(1024)(128)(4,1)}), s8[4194304]{0:T(1024)(128)(4,1)S(1)}, s32[]{:S(2)}) async-start(s8[10485760]{0:T(1024)(128)(4,1)} %bitcast.84), calls=%async_computation.5 | async-start | bytes 8388608
  712.5 15.3 %slice-start.2 = ((s8[10485760]{0:T(1024)(128)(4,1)}), s8[2097152]{0:T(1024)(128)(4,1)S(1)}, s32[]{:S(2)}) async-start(s8[10485760]{0:T(1024)(128)(4,1)} %bitcast.84), calls=%async_computation.6 | async-start | bytes 4194304
  (27 other events, 99.6 us)
Sparse Core Ops, SparseCore 0:
  129.7 45.3 all-reduce.7
  217.6 43.9 all-reduce.9
  363.5 292.6 all-reduce.11
  659.3 41.7 all-reduce.13
where the time goes:
time: 846 us; the launch traced here: 835 us
  waiting for transfers between devices  359 us (42%)
  matrix products  149 us (18%)
  local copies, waits for them, and re-layouts  142 us (17%)
  other arithmetic  92.2 us (11%)
  blocking collectives  78 us (9%)
  between operations  14.8 us (2%)
    psum x1, waiting for transfers between devices, body(): lax.psum(d_qkv.astype(jnp.bfloat16), 'dp').astype(jnp.float32)  264 us
    unnamed x122, local copies, waits for them, and re-layouts  82.1 us
    psum x1, blocking collectives, body(): lax.psum(d_table.astype(jnp.bfloat16), 'dp').astype(jnp.float32)  78 us
    psum x1, waiting for transfers between devices, body(): attn_full = lax.psum(attn_part, 'head')  45.5 us
    psum x1, waiting for transfers between devices, body(): lax.psum(down_part.astype(jnp.bfloat16), 'head').astype(jnp.float32)  32 us
    reshape x1, local copies, waits for them, and re-layouts, body(): proj = proj.reshape(items, span, 3, heads_here, HEAD_DIM)  23.8 us
    psum x1, waiting for transfers between devices, body(): h2_grad = lax.psum(h2_part, 'head')  17.3 us
  transfers between devices with their start and end apart: 4, of which 4 were waited for; matrix products, arithmetic and copies ran while one was open for 8% of the time, Pallas kernels for 0%

commit v1 on v0

--- a/solution.py
+++ b/solution.py
@@ -1,15 +1,796 @@
 from functools import partial
+
+import numpy as np
 
 import jax
 import jax.numpy as jnp
 from jax import lax
+from jax.experimental import pallas as pl
+from jax.experimental.pallas import tpu as pltpu
 from jax.sharding import PartitionSpec as P
 
 HEAD_DIM = 160
-
-
 EPS = 1e-05
+SCALE = HEAD_DIM ** (-0.5)
+LANE = 128
+WINDOW = 256
+VMEM = 36 * 2**20
+F32 = jnp.float32
+BF16 = jnp.bfloat16
+AXES = ("dp", "head")
 HIGH = lax.Precision.HIGHEST
+ROOT = 0.7978845608028654
+CUBE = 0.044715
+
+
+def dot(a, b):
+    return jnp.dot(a, b, preferred_element_type=F32)
+
+
+def dot_t(a, b):
+    return lax.dot_general(a, b, (((1,), (1,)), ((), ())), preferred_element_type=F32)
+
+
+def t_dot(a, b):
+    return lax.dot_general(a, b, (((0,), (0,)), ((), ())), preferred_element_type=F32)
+
+
+def row_mean(v):
+    return jnp.mean(v, axis=-1, keepdims=True)
+
+
+def unit_of(v):
+    centred = v - row_mean(v)
+    inverse = lax.rsqrt(row_mean(centred * centred) + EPS)
+    return centred * inverse, inverse
+
+
+def unit_back(grad, unit, inverse, gain):
+    scaled = grad * gain
+    return inverse * (scaled - row_mean(scaled) - unit * row_mean(scaled * unit))
+
+
+def column_sum(v):
+    return jnp.sum(v, axis=0, keepdims=True)
+
+
+def add_to(ref, value, first):
+    @pl.when(first)
+    def _():
+        ref[...] = value
+
+    @pl.when(jnp.logical_not(first))
+    def _():
+        ref[...] += value
+
+
+def table_row(tab_ref, lang):
+    table = tab_ref[...].astype(F32)
+    rows = lax.broadcasted_iota(jnp.int32, table.shape, 0)
+    return jnp.sum(jnp.where(rows == lang, table, 0.0), axis=0, keepdims=True)
+
+
+def lang_of(meta, side):
+    return meta[2 + meta[side] + pl.program_id(0)]
+
+
+def base_of(meta, lat_ref, tab_ref, side):
+    return lat_ref[...].astype(F32) + table_row(tab_ref, lang_of(meta, side))
+
+
+def head_mask(a):
+    lane = lax.broadcasted_iota(jnp.int32, (1, WINDOW), 1)
+    first = HEAD_DIM * a - LANE * a
+    return ((lane >= first) & (lane < first + HEAD_DIM)).astype(F32).astype(BF16)
+
+
+def join_heads(parts):
+    lane = lax.broadcasted_iota(jnp.int32, (parts[0].shape[0], LANE), 1)
+    blocks = [parts[0][:, :LANE]]
+    for b in range(1, len(parts)):
+        edge = HEAD_DIM * b - LANE * b
+        blocks.append(jnp.where(lane < edge, parts[b - 1][:, LANE:], parts[b][:, :LANE]))
+    blocks.append(parts[-1][:, LANE:])
+    return jnp.concatenate(blocks, axis=1)
+
+
+def windows(count):
+    return [slice(LANE * a, LANE * a + WINDOW) for a in range(count)]
+
+
+def attend_kernel(
+    meta,
+    lat_ref,
+    tab_ref,
+    gain_ref,
+    shift_ref,
+    w_ref,
+    h_ref,
+    proj_ref,
+    prob_ref,
+    mixed_ref,
+    *,
+    side,
+):
+    unit, _ = unit_of(base_of(meta, lat_ref, tab_ref, side))
+    hidden = (unit * gain_ref[...] + shift_ref[...]).astype(BF16)
+    h_ref[...] = hidden
+    for c in range(3):
+        proj_ref[c] = dot(hidden, w_ref[c]).astype(BF16)
+    lanes = windows(prob_ref.shape[1])
+    raw = [
+        dot_t(proj_ref[0, :, w] * head_mask(a), proj_ref[1, :, w]) for a, w in enumerate(lanes)
+    ]
+    low = []
+    for a, scores in enumerate(raw):
+        scores = scores * SCALE
+        weights = jnp.exp(scores - jnp.max(scores, axis=-1, keepdims=True))
+        probs = weights * (1.0 / jnp.sum(weights, axis=-1, keepdims=True))
+        low.append(probs.astype(BF16))
+        prob_ref[0, a] = low[a]
+    parts = [dot(low[a], proj_ref[2, :, w]) for a, w in enumerate(lanes)]
+    mixed_ref[...] = join_heads(parts).astype(BF16)
+
+
+def gelu(x):
+    square = x * x
+    tanh = jnp.tanh(x * (ROOT + (ROOT * CUBE) * square))
+    half = 0.5 + 0.5 * tanh
+    slope = half + x * (1.0 - tanh * tanh) * (0.5 * ROOT + (1.5 * ROOT * CUBE) * square)
+    return x * half, slope
+
+
+def feed_kernel(
+    meta,
+    lat_ref,
+    tab_ref,
+    cot_ref,
+    mix0_ref,
+    mix1_ref,
+    out0_ref,
+    out1_ref,
+    down0_ref,
+    down1_ref,
+    up0_ref,
+    up1_ref,
+    upb0_ref,
+    upb1_ref,
+    outb_ref,
+    downb_ref,
+    gain_ref,
+    shift_ref,
+    h_ref,
+    act0_ref,
+    act1_ref,
+    dpre0_ref,
+    dpre1_ref,
+    low_ref,
+    dmix0_ref,
+    dmix1_ref,
+    block_ref,
+    dgain_ref,
+    dshift_ref,
+    doutb_ref,
+    ddownb_ref,
+    dupb0_ref,
+    dupb1_ref,
+):
+    first = pl.program_id(0) == 0
+    base = base_of(meta, lat_ref, tab_ref, 0)
+    attn = dot(mix0_ref[...], out0_ref[...]) + dot(mix1_ref[...], out1_ref[...])
+    middle = base + attn + outb_ref[...]
+    cot = cot_ref[...]
+    d_act = (dot_t(cot, down0_ref[...]), dot_t(cot, down1_ref[...]))
+    unit, inverse = unit_of(middle)
+    hidden = (unit * gain_ref[...] + shift_ref[...]).astype(BF16)
+    h_ref[...] = hidden
+    pre = (dot(hidden, up0_ref[...]) + upb0_ref[...], dot(hidden, up1_ref[...]) + upb1_ref[...])
+    acts, d_pres = [], []
+    for j, (act_ref, dpre_ref, dupb_ref) in enumerate(
+        ((act0_ref, dpre0_ref, dupb0_ref), (act1_ref, dpre1_ref, dupb1_ref))
+    ):
+        act, slope = gelu(pre[j])
+        acts.append(act.astype(BF16))
+        d_pres.append((d_act[j] * slope).astype(BF16))
+        act_ref[...] = acts[j]
+        dpre_ref[...] = d_pres[j]
+        add_to(dupb_ref, column_sum(d_pres[j].astype(F32)), first)
+    grad = dot_t(d_pres[0], up0_ref[...]) + dot_t(d_pres[1], up1_ref[...])
+    out = dot(acts[0], down0_ref[...]) + dot(acts[1], down1_ref[...])
+    block_ref[...] = (middle + out + downb_ref[...]).astype(BF16)
+    cot = cot.astype(F32)
+    d_mid = cot + unit_back(grad, unit, inverse, gain_ref[...])
+    low = d_mid.astype(BF16)
+    low_ref[...] = low
+    dmix1_ref[...] = dot_t(low, out1_ref[...]).astype(BF16)
+    dmix0_ref[...] = dot_t(low, out0_ref[...]).astype(BF16)
+    add_to(dgain_ref, column_sum(grad * unit), first)
+    add_to(dshift_ref, column_sum(grad), first)
+    add_to(doutb_ref, column_sum(d_mid), first)
+    add_to(ddownb_ref, column_sum(cot), first)
+
+
+def put_pieces(piece, total, keep_ref, away_ref, table=0):
+    half, rows = keep_ref.shape[-3:-1]
+    groups = total.shape[0]
+    for s in range(half):
+        for ref, slot in ((keep_ref, s), (away_ref, s + half)):
+            p = piece[2 * half * table + slot]
+            start = pl.multiple_of(rows * (p // groups), 8)
+            ref[s] = total[p % groups, pl.ds(start, rows), :].astype(BF16)
+
+
+def attend_back_kernel(
+    piece,
+    h_ref,
+    proj_ref,
+    prob_ref,
+    dmixo_ref,
+    dmixp_ref,
+    dproj_ref,
+    *rest,
+    items,
+    each,
+):
+    outs, total = rest[:6], rest[6]
+    step = pl.program_id(0)
+    last = 2 * items // each - 1
+    own = step < items // each
+    span = proj_ref.shape[1] // each
+    d_all = jnp.where(own, dmixo_ref[...], dmixp_ref[...])
+    lanes = windows(prob_ref.shape[1])
+    for u in range(each):
+        rows = slice(span * u, span * u + span)
+        d_mixed = [d_all[rows, w] for w in lanes]
+        low = [prob_ref[u, a] for a in range(len(lanes))]
+        d_probs = [
+            dot_t(d_mixed[a] * head_mask(a), proj_ref[2, rows, w]) for a, w in enumerate(lanes)
+        ]
+        d_value = [t_dot(low[a], d_mixed[a]) for a in range(len(lanes))]
+        d_low = []
+        for a in range(len(lanes)):
+            probs = low[a].astype(F32)
+            d_raw = probs * (d_probs[a] - jnp.sum(probs * d_probs[a], axis=-1, keepdims=True))
+            d_low.append(d_raw.astype(BF16))
+        d_query = [dot(d_low[a], proj_ref[1, rows, w]) * SCALE for a, w in enumerate(lanes)]
+        d_key = [t_dot(d_low[a], proj_ref[0, rows, w]) * SCALE for a, w in enumerate(lanes)]
+        for c, parts in enumerate((d_query, d_key, d_value)):
+            dproj_ref[c, rows] = join_heads(parts).astype(BF16)
+
+    @pl.when(step == 0)
+    def _():
+        for c in range(3):
+            total[c] = t_dot(h_ref[...], dproj_ref[c])
+
+    @pl.when(step > 0)
+    def _():
+        for c in range(3):
+            total[c] += t_dot(h_ref[...], dproj_ref[c])
+
+    @pl.when(step == last)
+    def _():
+        for c in range(3):
+            put_pieces(piece, total.at[c : c + 1], outs[2 * c], outs[2 * c + 1], c)
+
+
+def hidden_grad_kernel(meta, dproj_ref, w_ref, out_ref):
+    grad = dot_t(dproj_ref[0], w_ref[0])
+    for c in range(1, 3):
+        grad += dot_t(dproj_ref[c], w_ref[c])
+    out_ref[...] = grad.astype(BF16)
+
+
+def base_grad_kernel(
+    meta,
+    lat_ref,
+    tab_ref,
+    low_ref,
+    part_ref,
+    dproj_ref,
+    w_ref,
+    gain_ref,
+    dbase_ref,
+    dgain_ref,
+    dshift_ref,
+    dtab_ref,
+):
+    first = pl.program_id(0) == 0
+    grad = part_ref[...].astype(F32)
+    for c in range(3):
+        grad += dot_t(dproj_ref[c], w_ref[c])
+    unit, inverse = unit_of(base_of(meta, lat_ref, tab_ref, 0))
+    d_base = low_ref[...].astype(F32) + unit_back(grad, unit, inverse, gain_ref[...])
+    dbase_ref[...] = d_base
+    add_to(dgain_ref, column_sum(grad * unit), first)
+    add_to(dshift_ref, column_sum(grad), first)
+
+    @pl.when(first)
+    def _():
+        dtab_ref[...] = jnp.zeros_like(dtab_ref)
+
+    lang = lang_of(meta, 0)
+    dtab_ref[pl.ds(lang, 1), :] += column_sum(d_base)
+
+
+def weight_grad_kernel(piece, a0_ref, a1_ref, b0_ref, b1_ref, keep_ref, away_ref, total):
+    step = pl.program_id(0)
+    groups, _, cols = total.shape
+    value = t_dot(a0_ref[...], b0_ref[...]) + t_dot(a1_ref[...], b1_ref[...])
+
+    @pl.when(step == 0)
+    def _():
+        for g in range(groups):
+            total[g] = value[:, cols * g : cols * g + cols]
+
+    @pl.when(step > 0)
+    def _():
+        for g in range(groups):
+            total[g] += value[:, cols * g : cols * g + cols]
+
+    @pl.when(step == pl.num_programs(0) - 1)
+    def _():
+        put_pieces(piece, total, keep_ref, away_ref)
+
+
+def plus(a, b):
+    return (a.astype(F32) + b.astype(F32)).astype(BF16)
+
+
+def finish_kernel(slot, near_ref, far_ref, out_ref):
+    half, rows, cols = near_ref.shape
+    groups = out_ref.shape[-1] // cols
+    for p in range(2 * half):
+        s = slot[p]
+        place = lax.rem(s, half)
+        value = jnp.where(
+            s < half, near_ref[place].astype(F32), far_ref[place].astype(F32)
+        )
+        r, g = p // groups, p % groups
+        out_ref[rows * r : rows * r + rows, cols * g : cols * g + cols] = value
+
+
+class Line:
+    def __init__(self):
+        self.last = None
+
+    def tie(self, *xs):
+        if self.last is not None:
+            *xs, self.last = lax.optimization_barrier((*xs, self.last))
+        return xs
+
+    def call(
+        self, kernel, scalars, grid, operands, outs, scratch=(), alias=None, vmem=VMEM, mark=-1
+    ):
+        arrays, in_specs = zip(*operands)
+        shapes, out_specs = zip(*outs)
+        (scalars,) = self.tie(scalars)
+        results = pl.pallas_call(
+            kernel,
+            out_shape=shapes,
+            grid_spec=pltpu.PrefetchScalarGridSpec(
+                num_scalar_prefetch=1,
+                grid=grid,
+                in_specs=in_specs,
+                out_specs=out_specs,
+                scratch_shapes=scratch,
+            ),
+            input_output_aliases=alias or {},
+            compiler_params=pltpu.CompilerParams(vmem_limit_bytes=vmem),
+            cost_estimate=pl.CostEstimate(flops=1, bytes_accessed=1, transcendentals=0),
+        )(scalars, *arrays)
+        if mark is not None:
+            self.last = results[mark]
+        return results
+
+
+def shaped(shape, dtype):
+    return jax.ShapeDtypeStruct(shape, dtype)
+
+
+def whole(x):
+    return (x, pl.BlockSpec(x.shape, lambda i, meta: (0,) * x.ndim, pipeline_mode=pl.Buffered(1)))
+
+
+def whole_out(shape, dtype):
+    return (shaped(shape, dtype), pl.BlockSpec(shape, lambda i, meta: (0,) * len(shape)))
+
+
+def any_place(x):
+    return (x, pl.BlockSpec(memory_space=pl.ANY))
+
+
+def row_blocks(x, span, first=0):
+    lead = x.shape[:-2]
+    spec = pl.BlockSpec(
+        lead + (span, x.shape[-1]), lambda i, meta: (0,) * len(lead) + (first + i, 0)
+    )
+    return (x, spec)
+
+
+def local_blocks(x, span, side):
+    return (x, pl.BlockSpec((span, x.shape[-1]), lambda i, meta: (meta[side] + i, 0)))
+
+
+def item_blocks(x, each=1, first=0):
+    lead = (0,) * (x.ndim - 1)
+    return (x, pl.BlockSpec((each,) + x.shape[1:], lambda i, meta: (first + i,) + lead))
+
+
+def swap(x):
+    return lax.ppermute(x, "head", [(0, 1), (1, 0)])
+
+
+class Sums:
+    def __init__(self, line, n_dp, n_head):
+        self.line, self.n_dp, self.n_head = line, n_dp, n_head
+        self.bits = n_dp.bit_length() - 1
+        self.me = lax.axis_index("dp")
+        self.head = lax.axis_index("head")
+        self.tables = {}
+
+    def order(self, *first):
+        bits = [b for b in first if b < self.bits]
+        bits += [b for b in range(self.bits) if b not in bits]
+        swapped = [{0: 1, 1: 0}.get(b, b) if self.bits > 1 else b for b in bits]
+        return (tuple(bits), tuple(swapped))
+
+    def table(self, order):
+        if order not in self.tables:
+            slots = np.arange(self.n_dp)
+            to_piece = np.zeros((self.n_head, self.n_dp), np.int32)
+            for h in range(self.n_head):
+                for s, bit in enumerate(order[h]):
+                    to_piece[h] |= ((slots >> (self.bits - 1 - s)) & 1) << bit
+            to_slot = np.argsort(to_piece, axis=1).astype(np.int32)
+            here = jnp.arange(self.n_dp, dtype=jnp.int32) ^ self.me
+            piece_of = jnp.where(self.head == 0, to_piece[0], to_piece[1]) ^ self.me
+            slot_of = jnp.where(
+                self.head == 0, jnp.asarray(to_slot[0])[here], jnp.asarray(to_slot[1])[here]
+            )
+            self.tables[order] = (piece_of.astype(jnp.int32), slot_of.astype(jnp.int32))
+        return self.tables[order]
+
+    def send(self, x, order, stage):
+        perm = []
+        for d in range(self.n_dp):
+            for h in range(self.n_head):
+                to = d ^ (1 << order[h][stage])
+                perm.append((d * self.n_head + h, to * self.n_head + h))
+        return lax.ppermute(x, AXES, perm)
+
+    def piece_shape(self, m, n):
+        return (m * n // (self.n_dp * 640), 640)
+
+    def halves_out(self, m, n):
+        return [whole_out((self.n_dp // 2,) + self.piece_shape(m, n), BF16)] * 2
+
+    def weight_grad(self, a0, a1, b0, b1, step, order):
+        rows, m = a0[0].shape
+        n = b0[0].shape[-1]
+        groups = n // 640
+        return self.line.call(
+            weight_grad_kernel,
+            jnp.concatenate([self.table(order)[0], self.meta]),
+            (rows // step,),
+            [a0, a1, b0, b1],
+            self.halves_out(m, n),
+            [pltpu.VMEM((groups, m, 640), F32)],
+        )
+
+    def reduce(self, keep, away, order, finish):
+        for stage in range(self.bits):
+            got = self.send(away, order, stage)
+            yield
+            keep, got = self.line.tie(keep, got)
+            half = keep.shape[0] // 2
+            if half:
+                keep, away = plus(keep[:half], got[:half]), plus(keep[half:], got[half:])
+                self.line.last = away
+            else:
+                keep = plus(keep, got)
+                self.line.last = keep
+        for stage in reversed(range(1, self.bits)):
+            got = self.send(keep, order, stage)
+            yield
+            keep, got = self.line.tie(keep, got)
+            keep = jnp.concatenate([keep, got], axis=0)
+            self.line.last = keep
+        got = self.send(keep, order, 0)
+        yield
+        finish(keep, got)
+        yield
+
+    def finish(self, near, far, order, shape):
+        (result,) = self.line.call(
+            finish_kernel,
+            self.table(order)[1],
+            (1,),
+            [whole(near), whole(far)],
+            [whole_out(shape, F32)],
+        )
+        return result
+
+    def finish3(self, parts, orders, shape):
+        scalars = jnp.concatenate([self.table(order)[1] for order in orders])
+        operands = [whole(x) for pair in parts for x in pair]
+
+        def kernel(slot, *refs):
+            out_ref = refs[-1]
+            for c in range(3):
+
+                @pl.when(pl.program_id(0) == c)
+                def _(c=c):
+                    finish_kernel(
+                        slot.at[pl.ds(self.n_dp * c, self.n_dp)],
+                        refs[2 * c],
+                        refs[2 * c + 1],
+                        out_ref.at[0],
+                    )
+
+        spec = pl.BlockSpec((1,) + shape[1:], lambda i, slot: (i, 0, 0))
+        (result,) = self.line.call(
+            kernel, scalars, (3,), operands, [(shaped(shape, F32), spec)], vmem=40 * 2**20
+        )
+        return result
+
+
+def sum_small(line, x, total, finish):
+    bit = 1
+    while bit < total:
+        got = lax.ppermute(x, AXES, [(i, i ^ bit) for i in range(total)])
+        yield
+        x, got = line.tie(x, got)
+        x = x + got
+        line.last = x
+        bit *= 2
+    finish(x)
+    yield
+
+
+def body(
+    latents,
+    languages,
+    lang_table,
+    norm1_gain,
+    norm1_shift,
+    qkv_weight,
+    out_weight,
+    out_bias,
+    norm2_gain,
+    norm2_shift,
+    up_weight,
+    up_bias,
+    down_weight,
+    down_bias,
+    cotangent,
+):
+    n_dp, n_head = lax.axis_size("dp"), lax.axis_size("head")
+    head = lax.axis_index("head")
+    width = latents.shape[1]
+    half = width // 2
+    heads = half // HEAD_DIM
+    span = latents.shape[0] // languages.shape[0]
+    rows = latents.shape[0] // 2
+    items = rows // span
+    starts = jnp.stack([head * items, (1 - head) * items]).astype(jnp.int32)
+    meta = jnp.concatenate([starts, languages.astype(jnp.int32)])
+    line = Line()
+    call = line.call
+    sums = Sums(line, n_dp, n_head)
+    sums.meta = starts
+    plane = sums.order(0, 1, 2, 3)
+    tall = sums.order(2, 0, 1, 3)
+    qkv_orders = (plane, plane, tall)
+
+    def one_row(v):
+        return v.reshape(1, -1)
+
+    qkv = jnp.transpose(qkv_weight, (1, 0, 2))
+    wo = (out_weight, swap(out_weight))
+    wu = (up_weight, swap(up_weight))
+    wd = (down_weight, swap(down_weight))
+    ub = (one_row(up_bias), one_row(swap(up_bias)))
+
+    lat = local_blocks(latents, span, 0)
+    cot = local_blocks(cotangent, span, 0)
+    tab = whole(lang_table)
+    gain1, shift1 = whole(one_row(norm1_gain)), whole(one_row(norm1_shift))
+    gain2, shift2 = whole(one_row(norm2_gain)), whole(one_row(norm2_shift))
+
+    def rows_out(cols, dtype, lead=()):
+        shape = shaped(lead + (rows, cols), dtype)
+        return (shape, row_blocks(shape, span)[1])
+
+    def sum_out(*shape):
+        return whole_out(shape, F32)
+
+    def half_out(shape, spec):
+        return (shape, spec)
+
+    grid = (items,)
+    h1_shape = shaped((2 * rows, width), BF16)
+    proj_shape = shaped((3, 2 * rows, half), BF16)
+    prob_shape = shaped((2 * items, heads, span, span), BF16)
+
+    def attend_side(side, into):
+        first = side * items
+        operands = [local_blocks(latents, span, side), tab, gain1, shift1, whole(qkv)]
+        alias = None
+        if into is not None:
+            operands += [any_place(x) for x in into]
+            alias = {1 + 5 + i: i for i in range(3)}
+
+        def kernel(meta, *refs):
+            attend_kernel(meta, *refs[:5], *refs[len(operands) :], side=side)
+
+        return call(
+            kernel,
+            meta,
+            grid,
+            operands,
+            [
+                row_blocks(h1_shape, span, first),
+                row_blocks(proj_shape, span, first),
+                item_blocks(prob_shape, 1, first),
+                rows_out(half, BF16),
+            ],
+            alias=alias,
+        )
+
+    h1, proj, prob, mixed_p = attend_side(1, None)
+    mixed_x = swap(mixed_p)
+    h1, proj, prob, mixed_o = attend_side(0, (h1, proj, prob))
+    h2, act0, act1, dpre0, dpre1, low, dmix0, dmix1, block_out, *sums2 = call(
+        feed_kernel,
+        meta,
+        grid,
+        [lat, tab, cot, row_blocks(mixed_o, span), row_blocks(mixed_x, span)]
+        + [whole(wo[0]), whole(wo[1]), whole(wd[0]), whole(wd[1]), whole(wu[0]), whole(wu[1])]
+        + [whole(ub[0]), whole(ub[1]), whole(one_row(out_bias)), whole(one_row(down_bias))]
+        + [gain2, shift2],
+        [rows_out(width, BF16)]
+        + [rows_out(half, BF16)] * 4
+        + [rows_out(width, BF16), rows_out(half, BF16), rows_out(half, BF16)]
+        + [rows_out(width, BF16)]
+        + [sum_out(1, width)] * 4
+        + [sum_out(1, half)] * 2,
+        vmem=58 * 2**20,
+        mark=0,
+    )
+    dgain2, dshift2, dbias, ddownb, dupb0, dupb1 = sums2
+    act_x = swap(act1)
+    dpre_x = swap(dpre1)
+    h2_x = swap(h2)
+    low_x = swap(low)
+    dmix_x = swap(dmix1)
+
+    step = min(rows, 512)
+    steps = rows // step
+
+    def shared(x, side):
+        return (
+            x,
+            pl.BlockSpec(
+                (step, x.shape[-1]), lambda i, s: (s[n_dp + side] * span // step + i, 0)
+            ),
+        )
+
+    def blocks(x):
+        return row_blocks(x, step)
+
+    results = {}
+
+    def keep_result(name, shape, order):
+        def finish(near, far):
+            results[name] = sums.finish(near, far, order, shape)
+
+        return finish
+
+    def keep_parts(c):
+        def finish(near, far):
+            results[c] = (near, far)
+
+        return finish
+
+    def advance(*chains):
+        for chain in chains:
+            next(chain)
+
+    keep, away = sums.weight_grad(
+        blocks(act0), blocks(act_x), shared(cotangent, 0), shared(cotangent, 1), step, plane
+    )
+    down = sums.reduce(keep, away, plane, keep_result("down", down_weight.shape, plane))
+    advance(down)
+    keep, away = sums.weight_grad(
+        blocks(h2), blocks(h2_x), blocks(dpre0), blocks(dpre_x), step, plane
+    )
+    up = sums.reduce(keep, away, plane, keep_result("up", up_weight.shape, plane))
+    advance(up, down)
+    keep, away = sums.weight_grad(
+        blocks(mixed_o), blocks(mixed_p), blocks(low), blocks(low_x), step, plane
+    )
+    out = sums.reduce(keep, away, plane, keep_result("out", out_weight.shape, plane))
+    advance(out, up, down)
+
+    each = 2 if items % 2 == 0 else 1
+    count = items // each
+    wide = each * span
+    qkv_halves = sums.halves_out(width, half)
+    dproj_shape = shaped((3, 2 * rows, half), BF16)
+    dmix_own = pl.BlockSpec((wide, half), lambda i, s: (jnp.minimum(i, count - 1), 0))
+    dmix_other = pl.BlockSpec((wide, half), lambda i, s: (jnp.maximum(i - count, 0), 0))
+    dproj, *pieces = call(
+        partial(attend_back_kernel, items=items, each=each),
+        jnp.concatenate([sums.table(order)[0] for order in qkv_orders]),
+        (2 * count,),
+        [row_blocks(h1, wide), row_blocks(proj, wide), item_blocks(prob, each)]
+        + [(dmix0, dmix_own), (dmix_x, dmix_other)],
+        [row_blocks(dproj_shape, wide)] + qkv_halves * 3,
+        [pltpu.VMEM((3, width, half), F32)],
+        vmem=50 * 2**20,
+        mark=0,
+    )
+    qkv_chains = [
+        sums.reduce(pieces[2 * c], pieces[2 * c + 1], qkv_orders[c], keep_parts(c))
+        for c in range(3)
+    ]
+    advance(*qkv_chains)
+    advance(out, up, down)
+    (part,) = call(
+        hidden_grad_kernel,
+        meta,
+        grid,
+        [row_blocks(dproj, span, items), whole(qkv)],
+        [rows_out(width, BF16)],
+    )
+    advance(out, up, down)
+    (part,) = line.tie(part)
+    part_x = swap(part)
+    advance(*qkv_chains)
+    advance(out, up, down)
+    dbase, dgain1, dshift1, dtab = call(
+        base_grad_kernel,
+        meta,
+        grid,
+        [lat, tab, row_blocks(low, span), row_blocks(part_x, span)]
+        + [row_blocks(dproj, span), whole(qkv), gain1],
+        [rows_out(width, F32), sum_out(1, width), sum_out(1, width)]
+        + [sum_out(*lang_table.shape)],
+    )
+    dupb = jnp.where(
+        head == 0,
+        jnp.concatenate([dupb0, dupb1], axis=1),
+        jnp.concatenate([dupb1, dupb0], axis=1),
+    )
+    small = jnp.concatenate([dtab, dgain1, dshift1, dbias, dgain2, dshift2, ddownb, dupb], axis=0)
+    small = sum_small(line, small, n_dp * n_head, lambda x: results.update(small=x))
+    chains = qkv_chains + [out, up, down, small]
+    live = list(chains)
+    while live:
+        for chain in list(live):
+            if next(chain, "end") == "end":
+                live.remove(chain)
+    dqkv = sums.finish3([results[c] for c in range(3)], qkv_orders, qkv.shape)
+    small = results["small"]
+    langs = lang_table.shape[0]
+    dgain1, dshift1, dbias, dgain2, dshift2, ddownb, dupb = [small[langs + i] for i in range(7)]
+    dupb = lax.dynamic_slice_in_dim(dupb, head * half, half, 0)
+    return (
+        block_out,
+        dbase,
+        small[:langs],
+        dgain1,
+        dshift1,
+        jnp.transpose(dqkv, (1, 0, 2)),
+        results["out"],
+        dbias,
+        dgain2,
+        dshift2,
+        results["up"],
+        dupb,
+        results["down"],
+        ddownb,
+    )
 
 
 def normalize(values, gain, shift):
@@ -33,7 +814,7 @@
     return lax.dynamic_slice_in_dim(values, start, share, 0)
 
 
-def body(
+def plain_body(
     latents,
     languages,
     lang_table,
@@ -208,4 +989,6 @@
         P("head", None),
         P(),
     )
-    return jax.shard_map(body, mesh=mesh, in_specs=in_specs, out_specs=out_specs, check_vma=False)
+    return jax.shard_map(
+        body if mesh.shape["head"] == 2 else plain_body,
+         mesh=mesh, in_specs=in_specs, out_specs=out_specs, check_vma=False)

time: 846 us -> 361 us (0.43)
  waiting for transfers between devices: 359 us -> 104 us
  matrix products: 149 us -> 0 us
  Pallas kernels: 0 us -> 146 us
  local copies, waits for them, and re-layouts: 142 us -> 32.9 us
  other arithmetic: 92.2 us -> 12.6 us
  blocking collectives: 78 us -> 0 us
  starting transfers between devices: 0.16 us -> 58.5 us
  between operations: 14.8 us -> 1.67 us
    psum x4 -> x0, waiting for transfers between devices: 359 us -> none  [the longest x1 264 us: body(): lax.psum(d_qkv.astype(jnp.bfloat16), 'dp').astype(jnp.float32)]
    dot_general x20 -> x0, matrix products: 149 us -> none  [the longest x1 16.7 us: body(): proj = jnp.dot(h_one, qkv_flat, preferred_element_type=f32).astype(bf16)]
    pallas_call x0 -> x13, Pallas kernels: none -> 146 us  [call(): pl.pallas_call(kernel, out_shape=shapes, grid_spec=pltpu.PrefetchScalarGr...]
    ppermute x0 -> x64, waiting for transfers between devices: none -> 104 us  [the longest x48 76 us: send(): return lax.ppermute(x, AXES, perm)]
    psum x1 -> x0, blocking collectives: 78 us -> none  [body(): lax.psum(d_table.astype(jnp.bfloat16), 'dp').astype(jnp.float32)]
    unnamed x122 -> x116, local copies, waits for them, and re-layouts: 82.1 us -> 21.8 us
    ppermute x0 -> x64, starting transfers between devices: none -> 58.5 us  [the longest x48 51.8 us: send(): return lax.ppermute(x, AXES, perm)]
    reduce_sum x8 -> x0, other arithmetic: 43.9 us -> none  [the longest x1 10.6 us: body(): d_gain2 = jnp.sum(h2_grad * unit2, axis=0)]
  transfers between devices with their start and end apart: 4 -> 64, of which waited for: 4 -> 24; matrix products, arithmetic and copies ran while one was open for 8% -> 7% of each run, Pallas kernels for 0% -> 28%
where the time goes in v1:
time: 361 us; the launch traced here: 356 us
  Pallas kernels  146 us (40%)
  waiting for transfers between devices  104 us (29%)
  starting transfers between devices  58.5 us (16%)
  local copies, waits for them, and re-layouts  32.9 us (9%)
  other arithmetic  12.6 us (3%)
    pallas_call x13, Pallas kernels, call(): pl.pallas_call(kernel, out_shape=shapes, grid_spec=pltpu.PrefetchScalarGr...  146 us
    ppermute x48, waiting for transfers between devices, send(): return lax.ppermute(x, AXES, perm)  76 us
    ppermute x48, starting transfers between devices, send(): return lax.ppermute(x, AXES, perm)  51.8 us
    unnamed x116, local copies, waits for them, and re-layouts  21.8 us
    ppermute x5, waiting for transfers between devices, sum_small(): got = lax.ppermute(x, AXES, [(i, i ^ bit) for i in range(total)])  18 us
    convert_element_type x24, other arithmetic, plus(): return (a.astype(F32) + b.astype(F32)).astype(BF16)  10.6 us
    ppermute x11, waiting for transfers between devices, swap(): return lax.ppermute(x, 'head', [(0, 1), (1, 0)])  9.79 us
  transfers between devices with their start and end apart: 64, of which 24 were waited for; matrix products, arithmetic and copies ran while one was open for 7% of the time, Pallas kernels for 28%

profile of v1, /device:TPU:0, one launch (start us, length us, event | category | flops | bytes accessed | tf_op | source)
XLA Modules:
  0.0 355.6 jit_solution(3273603306659852202)
XLA Ops:
  7.0 13.3 %shard_map.326 = (bf16[2048,1280]{1,0:T(8,128)(2,1)S(1)}, bf16[3,2048,640]{2,1,0:T(8,128)(2,1)}, bf16[8,4,256,256]{3,2,1,0:T(8,128)(2,1)S(1)}, bf16[1024,640]{1,0:T(8,128)(2,1)S(1)}) custom-call(s32[10]{0:T(128)S(1)} %pad_add_fusion.meta, bf16[2048,1280]{1,0:T(8,128)(2,1)} %lat_ref.3, bf16[16,1280]{1,0:T(8,128)(2,1)S(1)} %copy-done.15, ...), custom_call_target="tpu_custom_call" | custom-call | flops 1 | bytes 1 | tf_op jit(solution)/shard_map/pallas_call | solution.py:367
  20.8 13.3 %shard_map.327 = (bf16[2048,1280]{1,0:T(8,128)(2,1)S(1)}, bf16[3,2048,640]{2,1,0:T(8,128)(2,1)}, bf16[8,4,256,256]{3,2,1,0:T(8,128)(2,1)S(1)}, bf16[1024,640]{1,0:T(8,128)(2,1)S(1)}) custom-call(s32[10]{0:T(128)S(1)} %pad_add_fusion.meta, bf16[2048,1280]{1,0:T(8,128)(2,1)} %lat_ref.3, ...), custom_call_target="tpu_custom_call", output_to_operand_aliasing={{0}: (6, {}), {1}: (7, {}), {2}: (8, {})} | custom-call | flops 1 | bytes 1 | tf_op jit(solution)/shard_map/pallas_call | solution.py:367
  45.4 39.1 %shard_map.328 = (bf16[1024,1280]{1,0:T(8,128)(2,1)}, bf16[1024,640]{1,0:T(8,128)(2,1)}, bf16[1024,640]{1,0:T(8,128)(2,1)}, bf16[1024,640]{1,0:T(8,128)(2,1)}, b...) custom-call(s32[10]{0:T(128)} %copy-done.17, ...), custom_call_target="tpu_custom_call" | custom-call | flops 1 | bytes 1 | tf_op jit(solution)/shard_map/pallas_call | solution.py:367
  85.7 9.8 %collective-permute-done.5.a1_ref = bf16[1024,640]{1,0:T(8,128)(2,1)} collective-permute-done((bf16[1024,640]{1,0:T(8,128)(2,1)}, bf16[1024,640]{1,0:T(8,128)(2,1)}, u32[]{:S(2)}, u32[]{:S(2)}) %collective-permute-start.5) | collective-permute-done | bytes 1310752 | tf_op jit(solution)/shard_map/ppermute | solution.py:420
  99.2 6.4 %shard_map.329 = (bf16[8,80,640]{2,1,0:T(8,128)(2,1)S(1)}, bf16[8,80,640]{2,1,0:T(8,128)(2,1)S(1)}) custom-call(s32[18]{0:T(128)S(1)} %pad_add_fusion.1.piece, bf16[1024,640]{1,0:T(8,128)(2,1)S(1)} %copy-done.11, bf16[1024,640]{1,0:T(8,128)(2,1)} %collective-permute-done.5.a1_ref, bf16[2048,1280]{1,0:T(8,128)(2,1)S(1)} %copy-done.2, ...), custom_call_target="tpu_custom_call" | custom-call | flops 1 | bytes 1 | tf_op jit(solution)/shard_map/pallas_call | solution.py:367
  105.7 2.7 collective-permute-start.6
  108.4 8.0 %shard_map.330 = (bf16[8,80,640]{2,1,0:T(8,128)(2,1)S(1)}, bf16[8,80,640]{2,1,0:T(8,128)(2,1)S(1)}) custom-call(s32[18]{0:T(128)S(1)} %pad_add_fusion.1.piece, bf16[1024,1280]{1,0:T(8,128)(2,1)S(1)} %copy-done.10, bf16[1024,1280]{1,0:T(8,128)(2,1)} %collective-permute-done.7.a1_ref, bf16[1024,640]{1,0:T(8,128)(2,1)S(1)} %copy-done.14, ...), custom_call_target="tpu_custom_call" | custom-call | flops 1 | bytes 1 | tf_op jit(solution)/shard_map/pallas_call | solution.py:367
  121.1 5.1 %shard_map.331 = (bf16[8,80,640]{2,1,0:T(8,128)(2,1)S(1)}, bf16[8,80,640]{2,1,0:T(8,128)(2,1)S(1)}) custom-call(s32[18]{0:T(128)S(1)} %pad_add_fusion.1.piece, bf16[1024,640]{1,0:T(8,128)(2,1)S(1)} %copy-done.9, bf16[1024,640]{1,0:T(8,128)(2,1)S(1)} %copy-done.13, bf16[1024,1280]{1,0:T(8,128)(2,1)S(1)} %copy-done.6, ...), custom_call_target="tpu_custom_call" | custom-call | flops 1 | bytes 1 | tf_op jit(solution)/shard_map/pallas_call | solution.py:367
  127.8 5.4 %collective-permute-done.10 = bf16[8,80,640]{2,1,0:T(8,128)(2,1)S(1)} collective-permute-done((bf16[8,80,640]{2,1,0:T(8,128)(2,1)S(1)}, bf16[8,80,640]{2,1,0:T(8,128)(2,1)S(1)}, u32[]{:S(2)}, u32[]{:S(2)}) %collective-permute-start.10) | collective-permute-done | bytes 819232 | tf_op jit(solution)/shard_map/ppermute | solution.py:459
  137.8 25.2 %shard_map.332 = (bf16[3,2048,640]{2,1,0:T(8,128)(2,1)}, bf16[8,80,640]{2,1,0:T(8,128)(2,1)S(1)}, bf16[8,80,640]{2,1,0:T(8,128)(2,1)}, bf16[8,80,640]{2,1,0:T(8,...) custom-call(s32[48]{0:T(128)S(1)} %pad_add_fusion.2.piece, ...), custom_call_target="tpu_custom_call" | custom-call | flops 1 | bytes 1 | tf_op jit(solution)/shard_map/pallas_call | solution.py:367
  166.5 2.6 collective-permute-start.16
  169.2 3.2 copy-done.3
  172.4 8.8 %shard_map.333 = bf16[1024,1280]{1,0:T(8,128)(2,1)} custom-call(s32[10]{0:T(128)S(1)} %copy-done.18, bf16[3,2048,640]{2,1,0:T(8,128)(2,1)S(1)} %copy-done.3, bf16[3,1280,640]{2,1,0:T(8,128)(2,1)S(1)} %bitcast.12), custom_call_target="tpu_custom_call" | custom-call | flops 1 | bytes 1 | tf_op jit(solution)/shard_map/pallas_call | solution.py:367
  190.4 5.8 %collective-permute-done.24 = bf16[8,80,640]{2,1,0:T(8,128)(2,1)} collective-permute-done((bf16[8,80,640]{2,1,0:T(8,128)(2,1)}, bf16[8,80,640]{2,1,0:T(8,128)(2,1)}, u32[]{:S(2)}, u32[]{:S(2)}) %collective-permute-start.24) | collective-permute-done | bytes 819232 | tf_op jit(solution)/shard_map/ppermute | solution.py:459
  198.0 6.9 %collective-permute-done.23 = bf16[8,80,640]{2,1,0:T(8,128)(2,1)} collective-permute-done((bf16[8,80,640]{2,1,0:T(8,128)(2,1)}, bf16[8,80,640]{2,1,0:T(8,128)(2,1)}, u32[]{:S(2)}, u32[]{:S(2)}) %collective-permute-start.23) | collective-permute-done | bytes 819232 | tf_op jit(solution)/shard_map/ppermute | solution.py:459
  206.8 7.2 %collective-permute-done.22 = bf16[8,80,640]{2,1,0:T(8,128)(2,1)S(1)} collective-permute-done((bf16[8,80,640]{2,1,0:T(8,128)(2,1)}, bf16[8,80,640]{2,1,0:T(8,128)(2,1)S(1)}, u32[]{:S(2)}, u32[]{:S(2)}) %collective-permute-start.22) | collective-permute-done | bytes 819232 | tf_op jit(solution)/shard_map/ppermute | solution.py:459
  219.9 3.0 collective-permute-start.28
  225.3 13.0 %shard_map.334 = (f32[1024,1280]{1,0:T(8,128)}, f32[1,1280]{1,0:T(1,128)S(1)}, f32[1,1280]{1,0:T(1,128)S(1)}, f32[16,1280]{1,0:T(8,128)S(1)}) custom-call(s32[10]{0:T(128)S(1)} %copy-done.18, bf16[2048,1280]{1,0:T(8,128)(2,1)S(1)} %bitcast.7, bf16[16,1280]{1,0:T(8,128)(2,1)S(1)} %copy-done.16, bf16[1024,1280]{1,0:T(8,128)(2,1)S(1)} %copy-done.7, ...), custom_call_target="tpu_custom_call" | custom-call | flops 1 | bytes 1 | tf_op jit(solution)/shard_map/pallas_call | solution.py:367
  244.1 4.6 %collective-permute-done.27 = bf16[2,80,640]{2,1,0:T(8,128)(2,1)} collective-permute-done((bf16[2,80,640]{2,1,0:T(8,128)(2,1)S(1)}, bf16[2,80,640]{2,1,0:T(8,128)(2,1)}, u32[]{:S(2)}, u32[]{:S(2)}) %collective-permute-start.27) | collective-permute-done | bytes 204832 | tf_op jit(solution)/shard_map/ppermute | solution.py:459
  249.8 3.3 collective-permute-done.38
  256.7 3.0 collective-permute-start.43
  262.6 6.1 %collective-permute-done.44 = bf16[1,80,640]{2,1,0:T(8,128)(2,1)S(1)} collective-permute-done((bf16[1,80,640]{2,1,0:T(8,128)(2,1)S(1)}, bf16[1,80,640]{2,1,0:T(8,128)(2,1)S(1)}, u32[]{:S(2)}, u32[]{:S(2)}) %collective-permute-start.44) | collective-permute-done | bytes 102432 | tf_op jit(solution)/shard_map/ppermute | solution.py:459
  273.4 2.7 collective-permute-start.49
  276.5 5.8 %collective-permute-done.45.far_ref = bf16[8,80,640]{2,1,0:T(8,128)(2,1)S(1)} collective-permute-done((bf16[8,80,640]{2,1,0:T(8,128)(2,1)S(1)}, bf16[8,80,640]{2,1,0:T(8,128)(2,1)S(1)}, u32[]{:S(2)}, u32[]{:S(2)}) %collective-permute-start.45) | collective-permute-done | bytes 819232 | tf_op jit(solution)/shard_map/ppermute | solution.py:459
  282.8 2.6 shard_map.335
  289.2 5.1 %collective-permute-done.47 = bf16[4,80,640]{2,1,0:T(8,128)(2,1)S(1)} collective-permute-done((bf16[4,80,640]{2,1,0:T(8,128)(2,1)S(1)}, bf16[4,80,640]{2,1,0:T(8,128)(2,1)S(1)}, u32[]{:S(2)}, u32[]{:S(2)}) %collective-permute-start.47) | collective-permute-done | bytes 409632 | tf_op jit(solution)/shard_map/ppermute | solution.py:459
  299.3 2.6 shard_map.336
  307.2 3.2 collective-permute-done.56.far_ref
  310.4 2.6 shard_map.337
  314.6 8.7 %collective-permute-done.59 = bf16[4,80,640]{2,1,0:T(8,128)(2,1)S(1)} collective-permute-done((bf16[4,80,640]{2,1,0:T(8,128)(2,1)S(1)}, bf16[4,80,640]{2,1,0:T(8,128)(2,1)S(1)}, u32[]{:S(2)}, u32[]{:S(2)}) %collective-permute-start.59) | collective-permute-done | bytes 409632 | tf_op jit(solution)/shard_map/ppermute | solution.py:459
  328.4 18.0 %collective-permute-done.57 = f32[23,1280]{1,0:T(8,128)} collective-permute-done((f32[23,1280]{1,0:T(8,128)S(1)}, f32[23,1280]{1,0:T(8,128)}, u32[]{:S(2)}, u32[]{:S(2)}) %collective-permute-start.57) | collective-permute-done | bytes 117792 | tf_op jit(solution)/shard_map/ppermute | solution.py:540
  349.3 6.2 %shard_map.338 = f32[3,1280,640]{2,1,0:T(8,128)} custom-call(s32[48]{0:T(128)S(1)} %pad_add_fusion.3.slot, bf16[8,80,640]{2,1,0:T(8,128)(2,1)S(1)} %constant_dynamic-update-slice_fusion.30.refs_0_, bf16[8,80,640]{2,1,0:T(8,128)(2,1)} %collective-permute-done.61.refs_1_, bf16[8,80,640]{2,1,0:T(8,128)(2,1)S(1)} %constant_dynamic-update-slice_fusion.32.refs_2_, ...), custom_call_target="tpu_custom_call" | custom-call | flops 1 | bytes 1 | tf_op jit(solution)/shard_map/pallas_call | solution.py:367
  (300 shorter events, 100.9 us)
Async XLA Ops:
  0.6 42.6 %collective-permute-start.1 = (bf16[640,1280]{1,0:T(8,128)(2,1)}, bf16[640,1280]{1,0:T(8,128)(2,1)S(1)}, u32[]{:S(2)}, u32[]{:S(2)}) collective-permute-start(bf16[640,1280]{1,0:T(8,128)(2,1)} %out0_ref.1), channel_id=1, source_target_pairs={{0,1},{1,0},{2,3},{3,2},{4,5},{5,4},{6,7},{7,6},{8,9},{9,8},{10,11... | collective-permute-start | bytes 4915208 | tf_op jit(solution)/shard_map/ppermute | solution.py:420
  1.2 42.1 %collective-permute-start.2 = (bf16[640,1280]{1,0:T(8,128)(2,1)}, bf16[640,1280]{1,0:T(8,128)(2,1)S(1)}, u32[]{:S(2)}, u32[]{:S(2)}) collective-permute-start(bf16[640,1280]{1,0:T(8,128)(2,1)} %down0_ref.1), channel_id=1, source_target_pairs={{0,1},{1,0},{2,3},{3,2},{4,5},{5,4},{6,7},{7,6},{8,9},{9,8},{10,11... | collective-permute-start | bytes 4915208 | tf_op jit(solution)/shard_map/ppermute | solution.py:420
  1.2 42.1 %collective-permute-start.3 = (bf16[1280,640]{1,0:T(8,128)(2,1)}, bf16[1280,640]{1,0:T(8,128)(2,1)}, u32[]{:S(2)}, u32[]{:S(2)}) collective-permute-start(bf16[1280,640]{1,0:T(8,128)(2,1)} %up0_ref.1), channel_id=1, source_target_pairs={{0,1},{1,0},{2,3},{3,2},{4,5},{5,4},{6,7},{7,6},{8,9},{9,8},{10,11... | collective-permute-start | bytes 4915208 | tf_op jit(solution)/shard_map/ppermute | solution.py:420
  20.3 23.0 %collective-permute-start = (bf16[1024,640]{1,0:T(8,128)(2,1)S(1)}, bf16[1024,640]{1,0:T(8,128)(2,1)S(1)}, u32[]{:S(2)}, u32[]{:S(2)}) collective-permute-start(bf16[1024,640]{1,0:T(8,128)(2,1)S(1)} %get-tuple-element.161.a1_ref), channel_id=1, source_target_pairs={{0,1},{1,0},{2,3},{3,2},{4,5},{5,4},{6,7},{7,6},{8,9},{9,8},{10,11... | collective-permute-start | bytes 3932168 | tf_op jit(solution)/shard_map/ppermute | solution.py:420
  20.4 22.3 %collective-permute-start.4 = (f32[640]{0:T(1024)S(1)}, f32[640]{0:T(1024)S(1)}, u32[]{:S(2)}, u32[]{:S(2)}) collective-permute-start(f32[640]{0:T(1024)S(1)} %copy-done.38), channel_id=1, source_target_pairs={{0,1},{1,0},{2,3},{3,2},{4,5},{5,4},{6,7},{7,6},{8,9},{9,8},{10,11... | collective-permute-start | bytes 7688 | tf_op jit(solution)/shard_map/ppermute | solution.py:420
  84.5 23.9 %collective-permute-start.7 = (bf16[1024,1280]{1,0:T(8,128)(2,1)}, bf16[1024,1280]{1,0:T(8,128)(2,1)}, u32[]{:S(2)}, u32[]{:S(2)}) collective-permute-start(bf16[1024,1280]{1,0:T(8,128)(2,1)} %get-tuple-element.169.a0_ref), channel_id=1, source_target_pairs={{0,1},{1,0},{2,3},{3,2},{4,5},{5,4},{6,7},{7,6},{8,9},{9,8},{10,11... | collective-permute-start | bytes 7864328 | tf_op jit(solution)/shard_map/ppermute | solution.py:420
  84.6 36.4 %collective-permute-start.11 = (bf16[1024,1280]{1,0:T(8,128)(2,1)}, bf16[1024,1280]{1,0:T(8,128)(2,1)S(1)}, u32[]{:S(2)}, u32[]{:S(2)}) collective-permute-start(bf16[1024,1280]{1,0:T(8,128)(2,1)} %get-tuple-element.183.b0_ref.low_ref), channel_id=1, source_target_pairs={{0,1},{1,0},{2,3},{3,2},{4,5},{5,4},{6,7},{7,6},{8,9},{9,8},{10,11... | collective-permute-start | bytes 7864328 | tf_op jit(solution)/shard_map/ppermute | solution.py:420
  85.2 23.2 %collective-permute-start.8 = (bf16[1024,640]{1,0:T(8,128)(2,1)}, bf16[1024,640]{1,0:T(8,128)(2,1)}, u32[]{:S(2)}, u32[]{:S(2)}) collective-permute-start(bf16[1024,640]{1,0:T(8,128)(2,1)} %get-tuple-element.177), channel_id=1, source_target_pairs={{0,1},{1,0},{2,3},{3,2},{4,5},{5,4},{6,7},{7,6},{8,9},{9,8},{10,11... | collective-permute-start | bytes 3932168 | tf_op jit(solution)/shard_map/ppermute | solution.py:420
  116.4 16.8 %collective-permute-start.10 = (bf16[8,80,640]{2,1,0:T(8,128)(2,1)S(1)}, bf16[8,80,640]{2,1,0:T(8,128)(2,1)S(1)}, u32[]{:S(2)}, u32[]{:S(2)}) collective-permute-start(bf16[8,80,640]{2,1,0:T(8,128)(2,1)S(1)} %get-tuple-element.178), channel_id=1, source_target_pairs={{0,2},{1,5},{2,0},{3,7},{4,6},{5,1},{6,4},{7,3},{8,10},{9,13},{10,... | collective-permute-start | bytes 2457608 | tf_op jit(solution)/shard_map/ppermute | solution.py:459
  116.5 20.2 %collective-permute-start.15 = (bf16[1024,640]{1,0:T(8,128)(2,1)S(1)}, bf16[1024,640]{1,0:T(8,128)(2,1)S(1)}, u32[]{:S(2)}, u32[]{:S(2)}) collective-permute-start(bf16[1024,640]{1,0:T(8,128)(2,1)S(1)} %copy-done.44), channel_id=1, source_target_pairs={{0,1},{1,0},{2,3},{3,2},{4,5},{5,4},{6,7},{7,6},{8,9},{9,8},{10,11... | collective-permute-start | bytes 3932168 | tf_op jit(solution)/shard_map/ppermute | solution.py:420
  126.2 36.9 %collective-permute-start.14 = (bf16[8,80,640]{2,1,0:T(8,128)(2,1)S(1)}, bf16[8,80,640]{2,1,0:T(8,128)(2,1)S(1)}, u32[]{:S(2)}, u32[]{:S(2)}) collective-permute-start(bf16[8,80,640]{2,1,0:T(8,128)(2,1)S(1)} %get-tuple-element.184), channel_id=1, source_target_pairs={{0,2},{1,5},{2,0},{3,7},{4,6},{5,1},{6,4},{7,3},{8,10},{9,13},{10,... | collective-permute-start | bytes 2457608 | tf_op jit(solution)/shard_map/ppermute | solution.py:459
  133.4 30.5 %collective-permute-start.13 = (bf16[4,80,640]{2,1,0:T(8,128)(2,1)S(1)}, bf16[4,80,640]{2,1,0:T(8,128)(2,1)}, u32[]{:S(2)}, u32[]{:S(2)}) collective-permute-start(bf16[4,80,640]{2,1,0:T(8,128)(2,1)S(1)} %get-tuple-element.323), channel_id=1, source_target_pairs={{0,4},{1,3},{2,6},{3,1},{4,0},{5,7},{6,2},{7,5},{8,12},{9,11},{10,... | collective-permute-start | bytes 1228808 | tf_op jit(solution)/shard_map/ppermute | solution.py:459
  135.1 30.4 %collective-permute-start.12 = (bf16[2,80,640]{2,1,0:T(8,128)(2,1)S(1)}, bf16[2,80,640]{2,1,0:T(8,128)(2,1)}, u32[]{:S(2)}, u32[]{:S(2)}) collective-permute-start(bf16[2,80,640]{2,1,0:T(8,128)(2,1)S(1)} %get-tuple-element.336), channel_id=1, source_target_pairs={{0,8},{1,9},{2,10},{3,11},{4,12},{5,13},{6,14},{7,15},{8,0},{9,1},... | collective-permute-start | bytes 614408 | tf_op jit(solution)/shard_map/ppermute | solution.py:459
  163.3 18.0 %collective-permute-start.18 = (bf16[4,80,640]{2,1,0:T(8,128)(2,1)S(1)}, bf16[4,80,640]{2,1,0:T(8,128)(2,1)S(1)}, u32[]{:S(2)}, u32[]{:S(2)}) collective-permute-start(bf16[4,80,640]{2,1,0:T(8,128)(2,1)S(1)} %get-tuple-element.321), channel_id=1, source_target_pairs={{0,4},{1,3},{2,6},{3,1},{4,0},{5,7},{6,2},{7,5},{8,12},{9,11},{10,... | collective-permute-start | bytes 1228808 | tf_op jit(solution)/shard_map/ppermute | solution.py:459
  165.0 17.1 %collective-permute-start.17 = (bf16[2,80,640]{2,1,0:T(8,128)(2,1)S(1)}, bf16[2,80,640]{2,1,0:T(8,128)(2,1)S(1)}, u32[]{:S(2)}, u32[]{:S(2)}) collective-permute-start(bf16[2,80,640]{2,1,0:T(8,128)(2,1)S(1)} %get-tuple-element.335), channel_id=1, source_target_pairs={{0,8},{1,9},{2,10},{3,11},{4,12},{5,13},{6,14},{7,15},{8,0},{9,1},... | collective-permute-start | bytes 614408 | tf_op jit(solution)/shard_map/ppermute | solution.py:459
  166.5 16.4 %collective-permute-start.16 = (bf16[1,80,640]{2,1,0:T(8,128)(2,1)S(1)}, bf16[1,80,640]{2,1,0:T(8,128)(2,1)S(1)}, u32[]{:S(2)}, u32[]{:S(2)}) collective-permute-start(bf16[1,80,640]{2,1,0:T(8,128)(2,1)S(1)} %get-tuple-element.348), channel_id=1, source_target_pairs={{0,16},{1,17},{2,18},{3,19},{4,20},{5,21},{6,22},{7,23},{8,24},{9,... | collective-permute-start | bytes 307208 | tf_op jit(solution)/shard_map/ppermute | solution.py:459
  183.6 36.4 %collective-permute-start.25 = (bf16[1024,1280]{1,0:T(8,128)(2,1)}, bf16[1024,1280]{1,0:T(8,128)(2,1)}, u32[]{:S(2)}, u32[]{:S(2)}) collective-permute-start(bf16[1024,1280]{1,0:T(8,128)(2,1)} %shard_map.333), channel_id=1, source_target_pairs={{0,1},{1,0},{2,3},{3,2},{4,5},{5,4},{6,7},{7,6},{8,9},{9,8},{10,11... | collective-permute-start | bytes 7864328 | tf_op jit(solution)/shard_map/ppermute | solution.py:420
  184.3 20.7 %collective-permute-start.23 = (bf16[8,80,640]{2,1,0:T(8,128)(2,1)}, bf16[8,80,640]{2,1,0:T(8,128)(2,1)}, u32[]{:S(2)}, u32[]{:S(2)}) collective-permute-start(bf16[8,80,640]{2,1,0:T(8,128)(2,1)} %get-tuple-element.213), channel_id=1, source_target_pairs={{0,2},{1,5},{2,0},{3,7},{4,6},{5,1},{6,4},{7,3},{8,10},{9,13},{10,... | collective-permute-start | bytes 2457608 | tf_op jit(solution)/shard_map/ppermute | solution.py:459
  188.3 25.8 %collective-permute-start.22 = (bf16[8,80,640]{2,1,0:T(8,128)(2,1)}, bf16[8,80,640]{2,1,0:T(8,128)(2,1)S(1)}, u32[]{:S(2)}, u32[]{:S(2)}) collective-permute-start(bf16[8,80,640]{2,1,0:T(8,128)(2,1)} %get-tuple-element.211), channel_id=1, source_target_pairs={{0,8},{1,9},{2,10},{3,11},{4,12},{5,13},{6,14},{7,15},{8,0},{9,1},... | collective-permute-start | bytes 2457608 | tf_op jit(solution)/shard_map/ppermute | solution.py:459
  189.9 27.5 %collective-permute-start.21 = (bf16[2,80,640]{2,1,0:T(8,128)(2,1)}, bf16[2,80,640]{2,1,0:T(8,128)(2,1)S(1)}, u32[]{:S(2)}, u32[]{:S(2)}) collective-permute-start(bf16[2,80,640]{2,1,0:T(8,128)(2,1)} %get-tuple-element.333), channel_id=1, source_target_pairs={{0,8},{1,9},{2,10},{3,11},{4,12},{5,13},{6,14},{7,15},{8,0},{9,1},... | collective-permute-start | bytes 614408 | tf_op jit(solution)/shard_map/ppermute | solution.py:459
  196.2 22.8 %collective-permute-start.20 = (bf16[1,80,640]{2,1,0:T(8,128)(2,1)}, bf16[1,80,640]{2,1,0:T(8,128)(2,1)S(1)}, u32[]{:S(2)}, u32[]{:S(2)}) collective-permute-start(bf16[1,80,640]{2,1,0:T(8,128)(2,1)} %get-tuple-element.347), channel_id=1, source_target_pairs={{0,16},{1,17},{2,18},{3,19},{4,20},{5,21},{6,22},{7,23},{8,24},{9,... | collective-permute-start | bytes 307208 | tf_op jit(solution)/shard_map/ppermute | solution.py:459
  214.0 24.3 %collective-permute-start.32 = (bf16[4,80,640]{2,1,0:T(8,128)(2,1)S(1)}, bf16[4,80,640]{2,1,0:T(8,128)(2,1)S(1)}, u32[]{:S(2)}, u32[]{:S(2)}) collective-permute-start(bf16[4,80,640]{2,1,0:T(8,128)(2,1)S(1)} %get-tuple-element.315), channel_id=1, source_target_pairs={{0,4},{1,3},{2,6},{3,1},{4,0},{5,7},{6,2},{7,5},{8,12},{9,11},{10,... | collective-permute-start | bytes 1228808 | tf_op jit(solution)/shard_map/ppermute | solution.py:459
  217.4 21.1 %collective-permute-start.31 = (bf16[4,80,640]{2,1,0:T(8,128)(2,1)S(1)}, bf16[4,80,640]{2,1,0:T(8,128)(2,1)S(1)}, u32[]{:S(2)}, u32[]{:S(2)}) collective-permute-start(bf16[4,80,640]{2,1,0:T(8,128)(2,1)S(1)} %get-tuple-element.317), channel_id=1, source_target_pairs={{0,4},{1,3},{2,6},{3,1},{4,0},{5,7},{6,2},{7,5},{8,12},{9,11},{10,... | collective-permute-start | bytes 1228808 | tf_op jit(solution)/shard_map/ppermute | solution.py:459
  219.0 22.4 %collective-permute-start.30 = (bf16[4,80,640]{2,1,0:T(8,128)(2,1)S(1)}, bf16[4,80,640]{2,1,0:T(8,128)(2,1)S(1)}, u32[]{:S(2)}, u32[]{:S(2)}) collective-permute-start(bf16[4,80,640]{2,1,0:T(8,128)(2,1)S(1)} %get-tuple-element.319), channel_id=1, source_target_pairs={{0,2},{1,5},{2,0},{3,7},{4,6},{5,1},{6,4},{7,3},{8,10},{9,13},{10,... | collective-permute-start | bytes 1228808 | tf_op jit(solution)/shard_map/ppermute | solution.py:459
  219.8 21.7 %collective-permute-start.29 = (bf16[1,80,640]{2,1,0:T(8,128)(2,1)S(1)}, bf16[1,80,640]{2,1,0:T(8,128)(2,1)S(1)}, u32[]{:S(2)}, u32[]{:S(2)}) collective-permute-start(bf16[1,80,640]{2,1,0:T(8,128)(2,1)S(1)} %get-tuple-element.345), channel_id=1, source_target_pairs={{0,16},{1,17},{2,18},{3,19},{4,20},{5,21},{6,22},{7,23},{8,24},{9,... | collective-permute-start | bytes 307208 | tf_op jit(solution)/shard_map/ppermute | solution.py:459
  219.9 22.2 %collective-permute-start.28 = (bf16[1,80,640]{2,1,0:T(8,128)(2,1)S(1)}, bf16[1,80,640]{2,1,0:T(8,128)(2,1)S(1)}, u32[]{:S(2)}, u32[]{:S(2)}) collective-permute-start(bf16[1,80,640]{2,1,0:T(8,128)(2,1)S(1)} %add_convert_fusion.35), channel_id=1, source_target_pairs={{0,16},{1,17},{2,18},{3,19},{4,20},{5,21},{6,22},{7,23},{8,24},{9,... | collective-permute-start | bytes 307208 | tf_op jit(solution)/shard_map/ppermute | solution.py:459
  303.1 20.3 %collective-permute-start.59 = (bf16[4,80,640]{2,1,0:T(8,128)(2,1)S(1)}, bf16[4,80,640]{2,1,0:T(8,128)(2,1)S(1)}, u32[]{:S(2)}, u32[]{:S(2)}) collective-permute-start(bf16[4,80,640]{2,1,0:T(8,128)(2,1)S(1)} %constant_dynamic-update-slice_fusion.26), channel_id=1, source_target_pairs={{0,4},{1,3},{2,6},{3,1},{4,0},{5,7},{6,2},{7,5},{8,12},{9,11},{10,... | collective-permute-start | bytes 1228808 | tf_op jit(solution)/shard_map/ppermute | solution.py:459
  305.8 17.6 %collective-permute-start.58 = (bf16[4,80,640]{2,1,0:T(8,128)(2,1)S(1)}, bf16[4,80,640]{2,1,0:T(8,128)(2,1)S(1)}, u32[]{:S(2)}, u32[]{:S(2)}) collective-permute-start(bf16[4,80,640]{2,1,0:T(8,128)(2,1)S(1)} %constant_dynamic-update-slice_fusion.28), channel_id=1, source_target_pairs={{0,2},{1,5},{2,0},{3,7},{4,6},{5,1},{6,4},{7,3},{8,10},{9,13},{10,... | collective-permute-start | bytes 1228808 | tf_op jit(solution)/shard_map/ppermute | solution.py:459
  323.5 25.7 %collective-permute-start.63 = (bf16[8,80,640]{2,1,0:T(8,128)(2,1)S(1)}, bf16[8,80,640]{2,1,0:T(8,128)(2,1)S(1)}, u32[]{:S(2)}, u32[]{:S(2)}) collective-permute-start(bf16[8,80,640]{2,1,0:T(8,128)(2,1)S(1)} %constant_dynamic-update-slice_fusion.34.refs_4_), channel_id=1, source_target_pairs={{0,8},{1,9},{2,10},{3,11},{4,12},{5,13},{6,14},{7,15},{8,0},{9,1},... | collective-permute-start | bytes 2457608 | tf_op jit(solution)/shard_map/ppermute | solution.py:459
  325.3 23.9 %collective-permute-start.62 = (bf16[8,80,640]{2,1,0:T(8,128)(2,1)S(1)}, bf16[8,80,640]{2,1,0:T(8,128)(2,1)}, u32[]{:S(2)}, u32[]{:S(2)}) collective-permute-start(bf16[8,80,640]{2,1,0:T(8,128)(2,1)S(1)} %constant_dynamic-update-slice_fusion.32.refs_2_), channel_id=1, source_target_pairs={{0,2},{1,5},{2,0},{3,7},{4,6},{5,1},{6,4},{7,3},{8,10},{9,13},{10,... | collective-permute-start | bytes 2457608 | tf_op jit(solution)/shard_map/ppermute | solution.py:459
  326.7 22.6 %collective-permute-start.61 = (bf16[8,80,640]{2,1,0:T(8,128)(2,1)S(1)}, bf16[8,80,640]{2,1,0:T(8,128)(2,1)}, u32[]{:S(2)}, u32[]{:S(2)}) collective-permute-start(bf16[8,80,640]{2,1,0:T(8,128)(2,1)S(1)} %constant_dynamic-update-slice_fusion.30.refs_0_), channel_id=1, source_target_pairs={{0,2},{1,5},{2,0},{3,7},{4,6},{5,1},{6,4},{7,3},{8,10},{9,13},{10,... | collective-permute-start | bytes 2457608 | tf_op jit(solution)/shard_map/ppermute | solution.py:459
  327.3 19.0 %collective-permute-start.57 = (f32[23,1280]{1,0:T(8,128)S(1)}, f32[23,1280]{1,0:T(8,128)}, u32[]{:S(2)}, u32[]{:S(2)}) collective-permute-start(f32[23,1280]{1,0:T(8,128)S(1)} %add.203), channel_id=1, source_target_pairs={{0,16},{1,17},{2,18},{3,19},{4,20},{5,21},{6,22},{7,23},{8,24},{9,... | collective-permute-start | bytes 353288 | tf_op jit(solution)/shard_map/ppermute | solution.py:540
  (81 other events, 1011.4 us)
